TPU v7x, 32 devices: a whole 2x2x4 slice. The times are simulated.
32 devices in a mesh: dp: 16 (over z, y, x), tensor: 2 (over core).
Axes of the slice: x: 2, y: 2, z: 4, core: 2. Of those that a mesh axis runs over, the one named last changes fastest.
Arguments:
- hidden: bfloat16 [48, 256, 14336], P('dp', None, 'tensor'), may hold values from -6 to 6
- out_grad: bfloat16 [48, 256, 4096], P('dp', None, 'tensor'), may hold values from -0.29882812 to 0.29882812
- proj_in: bfloat16 [64, 14336], P(None, 'tensor'), may hold values from -0.046875 to 0.046875
- proj_out: bfloat16 [64, 4096], P(None, 'tensor'), may hold values from -0.09375 to 0.09375
- left_inv: float32 [64, 64], replicated, may hold values from -0.15 to 3, as said below
- right_inv: float32 [64, 64], replicated, may hold values from -0.15 to 3, as said below
- lengths: int32 [48], P('dp'), may hold values from 64 to 256
- language: int32 [48], P('dp'), may hold values from 0 to 99
- owner: int32 [100], replicated, may hold values from 0 to 15, as said below
Outputs:
- seq_grads: float32 [48, 4096], P('dp', 'tensor')
- owned_means: float32 [112, 4096], P('dp', 'tensor')
Inputs may be any that keep to these rules, and one draw needn't show every extreme that they name: `left_inv`: symmetric; diagonal entries 1 or more, off-diagonal entries of magnitude 0.15 or less. `right_inv`: symmetric; diagonal entries 1 or more, off-diagonal entries of magnitude 0.15 or less. Every owner holds 6 or 7 languages, and some owner holds 7.
All inputs are finite; a program needn't handle non-finite values.
Results may differ from a plain program's by a relative error of at most 0.0003.
Values sent between devices are 32-bit elements; how exact they have to be, the bound alone decides.
A program may use at most 64 MiB of HBM per device.

v0:
```python
import jax
import jax.numpy as jnp
from jax import lax
from jax.sharding import PartitionSpec as P


def project(values, projection):
    flattened = values.reshape(-1, values.shape[-1])
    return lax.dot_general(
        flattened, projection, (((1,), (1,)), ((), ())), preferred_element_type=jnp.float32
    )


def per_device(hidden, out_grad, proj_in, proj_out, left_inv, right_inv, lengths, language, owner):
    highest = lax.Precision.HIGHEST
    seq_count = hidden.shape[0]
    seq_length = hidden.shape[1]
    proj_rank = proj_in.shape[0]
    tensor_size = lax.axis_size("tensor")
    row_width = proj_rank // tensor_size
    row_start = lax.axis_index("tensor") * row_width
    left_part = project(hidden, proj_in)
    right_part = project(out_grad, proj_out)
    token_mask = (jnp.arange(seq_length, dtype=jnp.int32)[None, :] < lengths[:, None]).astype(
        jnp.float32
    )
    left_full, right_full = lax.psum((left_part, right_part), "tensor")
    left_full = left_full.reshape(seq_count, seq_length, proj_rank)
    right_full = right_full.reshape(seq_count, seq_length, proj_rank) * token_mask[:, :, None]
    full_grads = jnp.einsum("sti,stj->sij", left_full, right_full, precision=highest)
    left_done = jnp.einsum("ik,skj->sij", left_inv, full_grads, precision=highest)
    full_pre = jnp.einsum("sik,kj->sij", left_done, right_inv, precision=highest)
    grad_rows = lax.dynamic_slice_in_dim(full_grads, row_start, row_width, 1)
    pre_rows = lax.dynamic_slice_in_dim(full_pre, row_start, row_width, 1)
    grad_flat = grad_rows.reshape(seq_count, row_width * proj_rank)
    pre_flat = pre_rows.reshape(seq_count, row_width * proj_rank)
    lang_total = owner.shape[0]
    dp_size = lax.axis_size("dp")
    slot_count = (lang_total + dp_size - 1) // dp_size
    owned_rows = slot_count * dp_size
    lang_index = jnp.arange(lang_total, dtype=jnp.int32)
    same_owner = (owner[:, None] == owner[None, :]) & (lang_index[None, :] < lang_index[:, None])
    lang_slot = jnp.sum(same_owner.astype(jnp.int32), axis=1)
    lang_place = owner * slot_count + lang_slot
    lang_hot = (language[:, None] == lang_index[None, :]).astype(jnp.int32)
    seq_place = jnp.sum(lang_hot * lang_place[None, :], axis=1)
    place_hot = (seq_place[:, None] == jnp.arange(owned_rows, dtype=jnp.int32)[None, :]).astype(
        jnp.float32
    )
    slot_table = jnp.dot(place_hot.T, pre_flat, precision=highest)
    slot_counts = jnp.sum(place_hot, axis=0)
    summed, counted = (
        lax.psum_scatter(slot_table, "dp", scatter_dimension=0, tiled=True),
        lax.psum_scatter(slot_counts, "dp", scatter_dimension=0, tiled=True),
    )
    owned_means = summed / jnp.maximum(counted, 1.0)[:, None]
    return (grad_flat, owned_means)


def solution(mesh):
    return jax.shard_map(
        per_device,
        mesh=mesh,
        in_specs=(
            P("dp", None, "tensor"),
            P("dp", None, "tensor"),
            P(None, "tensor"),
            P(None, "tensor"),
            P(),
            P(),
            P("dp"),
            P("dp"),
            P(),
        ),
        out_specs=(P("dp", "tensor"), P("dp", "tensor")),
        check_vma=False,
    )
```

profile of v0, /device:TPU:0, one launch (start us, length us, event | category | flops | bytes accessed | tf_op | source)
XLA Modules:
  0.0 131.1 jit_solution(9801122916708472731)
XLA Ops:
  7.2 0.0 copy-start
  7.2 0.0 copy-start.5
  7.2 0.0 copy-start.7
  7.2 0.0 copy-start.8
  7.2 0.0 copy-start.6
  7.2 0.0 copy-start.3
  7.2 0.0 copy-start.4
  7.2 0.0 all-reduce.6.cloned.1.call-start
  7.3 0.0 copy-start.1
  7.3 7.9 %fusion.11 = f32[768,64]{0,1:T(8,128)S(1)} fusion(bf16[768,7168]{1,0:T(8,128)(2,1)} %bitcast.28, bf16[64,7168]{1,0:T(8,128)(2,1)} %param.11), kind=kOutput, calls=%fused_computation.25 | convolution fusion | flops 704643072 | bytes 12124160 | tf_op jit(solution)/shard_map/dot_general | solution.py:9
  15.2 0.7 copy.29
  15.9 0.0 copy-done
  15.9 0.0 copy-done.1
  15.9 1.1 fusion.12
  17.0 0.8 reshape.53
  17.8 0.0 all-reduce.6.cloned.1.call-update
  17.8 0.0 copy-done.7
  17.8 0.2 convert_reduce_fusion
  18.0 0.0 copy-done.8
  18.0 0.2 select_reduce_fusion
  18.2 0.1 convert_reduce_fusion.1
  18.3 0.0 copy-done.5
  18.3 0.6 fusion.10
  20.2 43.6 %all-reduce.1 = f32[112]{0:T(128)S(1)} all-reduce(f32[112]{0:T(128)S(1)} %convert_reduce_fusion.1), channel_id=3, replica_groups=mesh['dp'=16,'tensor'=2] {'dp'}, use_global_device_ids=true, to_apply=%region_6.0.clone | all-reduce | flops 112 | bytes 896
  63.8 0.1 dynamic-slice_maximum_fusion
  63.9 0.0 copy-done.6
  63.9 0.1 fusion.7
  63.9 0.0 all-reduce.6.cloned.1.call-done
  63.9 1.0 broadcast_multiply_fusion
  64.9 1.3 fusion.1
  66.2 0.0 copy-done.3
  66.2 0.3 convolution_bitcast_fusion
  66.6 0.0 copy-done.4
  66.6 0.3 fusion.4
  66.9 0.1 reshape.55
  67.0 1.6 %fusion.8 = f32[112,2048]{1,0:T(8,128)} fusion(f32[3,2048]{1,0:T(4,128)S(1)} %reshape.55, s32[3]{0:T(128)S(1)} %select_reduce_fusion), kind=kOutput, calls=%fused_computation.16 | convolution fusion | flops 8257872 | bytes 942092 | tf_op jit(solution)/shard_map/dot_general | solution.py:50
  68.6 44.9 %fusion = f32[8,2048]{1,0:T(8,128)S(1)} fusion(f32[112,2048]{1,0:T(8,128)} %fusion.8), kind=kCustom, calls=%all-reduce-scatter | all-reduce-scatter fusion | flops 262145 | bytes 983552
  113.5 4.3 %collective-permute-start = (f32[8,2048]{1,0:T(8,128)S(1)}, f32[8,2048]{1,0:T(8,128)}, u32[]{:S(2)}, u32[]{:S(2)}) collective-permute-start(f32[8,2048]{1,0:T(8,128)S(1)} %fusion), channel_id=1, source_target_pairs={{0,2},{2,4},{4,6},{6,8},{8,10},{10,12},{12,14},{14,16},{16,18},{18... | collective-permute-start | bytes 196616
  117.8 1.3 collective-permute-start.1
  119.1 0.7 reshape.54
  119.8 1.2 collective-permute-done.1
  121.0 0.0 copy-start.2
  121.0 0.6 copy-done.2
  121.6 0.0 collective-permute-done
  121.6 1.9 %concatenate = f32[23,2048]{1,0:T(8,128)S(1)} concatenate(f32[7,2048]{1,0:T(8,128)} %copy-done.2, f32[8,2048]{1,0:T(8,128)} %collective-permute-done, f32[8,2048]{1,0:T(8,128)S(1)} %fusion), dimensions={0} | concatenate | bytes 376832
  123.6 0.7 dynamic-slice_divide_fusion
  (4 shorter events, 0.0 us)
Async XLA Ops:
  7.2 8.7 %copy-start = (bf16[3,256,2048]{2,1,0:T(8,128)(2,1)S(1)}, bf16[3,256,2048]{2,1,0:T(8,128)(2,1)}, u32[]{:S(2)}) copy-start(bf16[3,256,2048]{2,1,0:T(8,128)(2,1)} %param.10) | copy-start | bytes 9437188
  7.2 11.1 %copy-start.5 = (u32[32]{0:T(128)S(1)}, u32[32]{0:T(128)}, u32[]{:S(2)}) copy-start(u32[32]{0:T(128)} %constant.23) | copy-start | bytes 388
  7.2 10.6 %copy-start.7 = (s32[100]{0:T(128)S(1)}, s32[100]{0:T(128)}, u32[]{:S(2)}) copy-start(s32[100]{0:T(128)} %param.17) | copy-start | bytes 1204
  7.2 10.8 %copy-start.8 = (s32[3]{0:T(128)S(1)}, s32[3]{0:T(128)}, u32[]{:S(2)}) copy-start(s32[3]{0:T(128)} %param.16) | copy-start | bytes 40
  7.2 56.7 %copy-start.6 = (s32[3]{0:T(128)S(1)}, s32[3]{0:T(128)}, u32[]{:S(2)}) copy-start(s32[3]{0:T(128)} %param.15) | copy-start | bytes 40
  7.2 59.0 %copy-start.3 = (f32[64,64]{1,0:T(8,128)S(1)}, f32[64,64]{1,0:T(8,128)}, u32[]{:S(2)}) copy-start(f32[64,64]{1,0:T(8,128)} %param.13) | copy-start | bytes 49156
  7.2 59.3 %copy-start.4 = (f32[64,64]{1,0:T(8,128)S(1)}, f32[64,64]{1,0:T(8,128)}, u32[]{:S(2)}) copy-start(f32[64,64]{1,0:T(8,128)} %param.14) | copy-start | bytes 49156
  7.2 56.7 %all-reduce.6.cloned.1.call-start = ((), (), s32[]{:S(2)}) async-start(), calls=%async_computation | async-start | bytes 917504 | tf_op jit(solution)/shard_map/psum | solution.py:27
  7.3 8.6 %copy-start.1 = (bf16[64,2048]{1,0:T(8,128)(2,1)S(1)}, bf16[64,2048]{1,0:T(8,128)(2,1)}, u32[]{:S(2)}) copy-start(bf16[64,2048]{1,0:T(8,128)(2,1)} %param.12) | copy-start | bytes 786436
  113.5 8.1 %collective-permute-start = (f32[8,2048]{1,0:T(8,128)S(1)}, f32[8,2048]{1,0:T(8,128)}, u32[]{:S(2)}, u32[]{:S(2)}) collective-permute-start(f32[8,2048]{1,0:T(8,128)S(1)} %fusion), channel_id=1, source_target_pairs={{0,2},{2,4},{4,6},{6,8},{8,10},{10,12},{12,14},{14,16},{16,18},{18... | collective-permute-start | bytes 196616
  117.8 3.2 %collective-permute-start.1 = (f32[7,2048]{1,0:T(8,128)S(1)}, f32[7,2048]{1,0:T(8,128)S(1)}, u32[]{:S(2)}, u32[]{:S(2)}) collective-permute-start(f32[7,2048]{1,0:T(8,128)S(1)} %slice), channel_id=1, source_target_pairs={{0,4},{2,6},{4,8},{6,10},{8,12},{10,14},{12,16},{14,18},{16,20},{1... | collective-permute-start | bytes 172040
  121.0 0.6 copy-start.2
Sparse Core Ops, SparseCore 0:
  18.0 21.3 all-reduce.5
where the time goes:
time: 132 us; the launch traced here: 131 us
  blocking collectives  88.5 us (67%)
  between operations  15.5 us (12%)
  matrix products  12.5 us (9%)
  starting transfers between devices  5.58 us (4%)
  local copies, waits for them, and re-layouts  5.54 us (4%)
  other arithmetic  2.31 us (2%)
    unnamed x2, blocking collectives  88.5 us
    dot_general x2, matrix products, project(): lax.dot_general(flattened, projection, (((1,), (1,)), ((), ())), preferre...  9 us
    unnamed x2, starting transfers between devices  5.54 us
    unnamed x21, local copies, waits for them, and re-layouts  3.21 us
  transfers between devices with their start and end apart: 3, of which 1 were waited for; matrix products, arithmetic and copies ran while one was open for 1% of the time, Pallas kernels for 0%

commit v1 on v0

v1 whole, which is shorter than its diff:
```python
import functools
import math

import jax
import jax.numpy as jnp
from jax import lax
from jax.experimental import pallas as pl
from jax.experimental.pallas import tpu as pltpu
from jax.sharding import PartitionSpec as P

LANES = 128
HIGHEST = lax.Precision.HIGHEST


def pieces_of(width):
    for count in (4, 2):
        if width % (count * 256) == 0:
            return count
    return 1


def kernel(
    sizes,
    lengths,
    language,
    owner_list,
    owner_row,
    left_inv,
    right_inv,
    hidden,
    out_grad,
    proj_in,
    proj_out,
    grads_out,
    means_out,
    hid,
    og,
    w_in,
    w_out,
    part,
    peer_part,
    g_scr,
    gathered,
    places,
    hid_sem,
    og_sem,
    w_sem,
    t_send,
    t_recv,
    z_send,
    z_recv,
    p_send,
    p_recv,
    m_send,
    m_recv,
):
    t_size, outer, inner, slots = sizes
    seqs, tokens, hid_width = hid.shape
    rank = w_in.shape[0]
    half = rank // t_size
    rows = half // 2
    dp = lax.axis_index("dp")
    t_me = lax.axis_index("tensor")
    my_out = dp // inner
    my_in = dp % inner
    hid_pieces = pieces_of(hid_width)
    piece = hid_width // hid_pieces

    w_in_copy = pltpu.make_async_copy(proj_in, w_in, w_sem.at[0])
    w_out_copy = pltpu.make_async_copy(proj_out, w_out, w_sem.at[1])
    w_out_copy.start()
    og_copies = []
    hid_copies = []
    for s in range(seqs):
        og_copies.append(pltpu.make_async_copy(out_grad.at[s], og.at[s], og_sem.at[s]))
        og_copies[s].start()
        if s == 0:
            w_in_copy.start()
        for c in range(hid_pieces):
            cols = pl.ds(c * piece, piece)
            hid_copies.append(
                pltpu.make_async_copy(
                    hidden.at[s, :, cols], hid.at[s, :, cols], hid_sem.at[s, c]
                )
            )
            hid_copies[-1].start()

    def t_peer(k):
        return (dp, (t_me + k) % t_size)

    def z_peer(k):
        return (((my_out + k) % outer) * inner + my_in, t_me)

    def p_peer(k):
        return (my_out * inner + (my_in + k) % inner, t_me)

    peers = [(t_peer, t_size), (z_peer, outer), (p_peer, inner)]
    barrier = pltpu.get_barrier_semaphore()
    for peer_of, count in peers:
        for k in range(1, count):
            pl.semaphore_signal(
                barrier, inc=1, device_id=peer_of(k), device_id_type=pl.DeviceIdType.MESH
            )

    own_row = owner_row[...]
    lang_lane = lax.broadcasted_iota(jnp.int32, own_row.shape, 1)
    sub = lax.broadcasted_iota(jnp.int32, places.shape[2:], 0)
    place_block = jnp.full(places.shape[2:], -1, jnp.int32)
    for s in range(seqs):
        lang = language[s]
        own = owner_list[lang]
        earlier = (own_row == own) & (lang_lane < lang)
        slot = jnp.sum(earlier.astype(jnp.int32), axis=1, keepdims=True)
        place_block = jnp.where(sub == s, own * slots + slot, place_block)
    places[my_in, my_out] = place_block

    def send(src, dst, send_sem, recv_sem, peer):
        pltpu.make_async_remote_copy(
            src_ref=src,
            dst_ref=dst,
            send_sem=send_sem,
            recv_sem=recv_sem,
            device_id=peer,
            device_id_type=pl.DeviceIdType.MESH,
        ).start()

    def take(block, sem):
        pltpu.make_async_copy(block, block, sem).wait()

    def project(s):
        og_copies[s].wait()
        dims = (((1,), (1,)), ((), ()))
        right = lax.dot_general(og[s], w_out[...], dims, preferred_element_type=jnp.float32)
        left = jnp.zeros((tokens, rank), jnp.float32)
        for c in range(hid_pieces):
            if s == 0 and c == 0:
                w_in_copy.wait()
            hid_copies[s * hid_pieces + c].wait()
            cols = slice(c * piece, (c + 1) * piece)
            left += lax.dot_general(
                hid[s, :, cols], w_in[:, cols], dims, preferred_element_type=jnp.float32
            )
        part[s] = jnp.concatenate([left, right], axis=1)

    def send_part(s):
        for k in range(1, t_size):
            send(part.at[s], peer_part.at[s, k - 1], t_send.at[s], t_recv.at[s], t_peer(k))

    first = t_me * half
    even = pl.ds(first, rows, stride=2)
    odd = pl.ds(first + 1, rows, stride=2)

    def reduce(s):
        if t_size > 1:
            take(peer_part.at[s], t_recv.at[s])
        both = part[s]
        for k in range(1, t_size):
            both += peer_part[s, k - 1]
        token = lax.broadcasted_iota(jnp.int32, both.shape, 0)
        both = jnp.where(token < lengths[s], both, 0.0)
        high = both.astype(jnp.bfloat16)
        low = (both - high.astype(jnp.float32)).astype(jnp.bfloat16)
        split = jnp.concatenate([high, low], axis=1)
        full = lax.dot_general(
            split, split, (((0,), (0,)), ((), ())), preferred_element_type=jnp.float32
        )
        wide = 2 * rank
        full = full[0:rank] + full[wide : wide + rank]
        full = full[:, 0:wide] + full[:, wide : 2 * wide]
        grads = full[:, rank:wide]
        g_scr[s] = grads
        left_rows = jnp.concatenate([left_inv[even, :], left_inv[odd, :]], axis=0)
        done = jnp.dot(left_rows, grads, precision=HIGHEST, preferred_element_type=jnp.float32)
        pre = jnp.dot(
            done, right_inv[...], precision=HIGHEST, preferred_element_type=jnp.float32
        )
        gathered[s, my_in, my_out] = jnp.concatenate([pre[:rows], pre[rows:]], axis=1)
        for k in range(1, outer):
            block = gathered.at[s, my_in, my_out]
            send(block, block, z_send.at[s], z_recv.at[s], z_peer(k))
        pair = jnp.concatenate([g_scr[s, even, :], g_scr[s, odd, :]], axis=1)
        for r in range(rows):
            grads_out[s : s + 1, r * LANES : (r + 1) * LANES] = pair[r : r + 1]

    def forward(s):
        if s == 0:
            if outer > 1:
                take(places.at[0, pl.ds(0, outer - 1)], m_recv.at[0])
            for k in range(1, inner):
                block = places.at[my_in]
                send(block, block, m_send.at[1], m_recv.at[1], p_peer(k))
        if outer > 1:
            take(gathered.at[s, 0, pl.ds(0, outer - 1)], z_recv.at[s])
        for k in range(1, inner):
            block = gathered.at[s, my_in]
            send(block, block, p_send.at[s], p_recv.at[s], p_peer(k))

    def accumulate(s, held):
        if s == 0 and inner > 1:
            take(places.at[pl.ds(0, inner - 1)], m_recv.at[1])
        if inner > 1:
            take(gathered.at[s, pl.ds(0, inner - 1)], p_recv.at[s])

        def step(i, held):
            sums, counts = held
            sums, counts = list(sums), list(counts)
            for o in range(outer):
                place = places[i, o, s : s + 1, :]
                row = gathered[s, i, o]
                for j in range(slots):
                    hit = (place == dp * slots + j).astype(jnp.float32)
                    sums[j] = sums[j] + hit * row
                    counts[j] = counts[j] + hit
            return tuple(sums), tuple(counts)

        return lax.fori_loop(0, inner, step, held)

    w_out_copy.wait()
    for s in range(seqs):
        project(s)
        if s == 0:
            pl.semaphore_wait(barrier, sum(count - 1 for _, count in peers))
            for k in range(1, outer):
                block = places.at[my_in, my_out]
                send(block, block, m_send.at[0], m_recv.at[0], z_peer(k))
        send_part(s)
        if s >= 2:
            forward(s - 2)
        if s >= 1:
            reduce(s - 1)
    if seqs >= 2:
        forward(seqs - 2)
    reduce(seqs - 1)
    held = (
        tuple(jnp.zeros((rows, LANES), jnp.float32) for _ in range(slots)),
        tuple(jnp.zeros((1, LANES), jnp.float32) for _ in range(slots)),
    )
    for s in range(seqs - 2):
        held = accumulate(s, held)
    forward(seqs - 1)
    for s in range(max(seqs - 2, 0), seqs):
        held = accumulate(s, held)
    sums, counts = held
    for j in range(slots):
        mean = sums[j] / jnp.maximum(counts[j], 1.0)
        for r in range(rows):
            means_out[j : j + 1, r * LANES : (r + 1) * LANES] = mean[r : r + 1]

    for s in range(seqs):
        if t_size > 1:
            take(peer_part.at[s], t_send.at[s])
        if outer > 1:
            take(gathered.at[s, 0, pl.ds(0, outer - 1)], z_send.at[s])
        if inner > 1:
            take(gathered.at[s, pl.ds(0, inner - 1)], p_send.at[s])
    if outer > 1:
        take(places.at[0, pl.ds(0, outer - 1)], m_send.at[0])
    if inner > 1:
        take(places.at[pl.ds(0, inner - 1)], m_send.at[1])


def per_device(hidden, out_grad, proj_in, proj_out, left_inv, right_inv, lengths, language, owner):
    seqs, tokens, hid_width = hidden.shape
    og_width = out_grad.shape[2]
    rank = proj_in.shape[0]
    t_size = lax.axis_size("tensor")
    dp_size = lax.axis_size("dp")
    inner = 2 ** (int(math.log2(dp_size)) // 2)
    while dp_size % inner:
        inner -= 1
    outer = dp_size // inner
    slots = (owner.shape[0] + dp_size - 1) // dp_size
    half = rank // t_size
    rows = half * rank // LANES
    smem = pl.BlockSpec(memory_space=pltpu.SMEM)
    vmem = pl.BlockSpec(memory_space=pltpu.VMEM)
    anywhere = pl.BlockSpec(memory_space=pl.ANY)
    dma = pltpu.SemaphoreType.DMA
    flops = 2 * seqs * tokens * rank * (hid_width + og_width)
    return pl.pallas_call(
        functools.partial(kernel, (t_size, outer, inner, slots)),
        out_shape=(
            jax.ShapeDtypeStruct((seqs, half * rank), jnp.float32),
            jax.ShapeDtypeStruct((slots, half * rank), jnp.float32),
        ),
        in_specs=[smem, smem, smem, vmem, vmem, vmem] + [anywhere] * 4,
        out_specs=(vmem, vmem),
        scratch_shapes=[
            pltpu.VMEM((seqs, tokens, hid_width), jnp.bfloat16),
            pltpu.VMEM((seqs, tokens, og_width), jnp.bfloat16),
            pltpu.VMEM((rank, hid_width), jnp.bfloat16),
            pltpu.VMEM((rank, og_width), jnp.bfloat16),
            pltpu.VMEM((seqs, tokens, 2 * rank), jnp.float32),
            pltpu.VMEM((seqs, max(t_size - 1, 1), tokens, 2 * rank), jnp.float32),
            pltpu.VMEM((seqs, rank, rank), jnp.float32),
            pltpu.VMEM((seqs, inner, outer, rows, LANES), jnp.float32),
            pltpu.VMEM((inner, outer, 8 * ((seqs + 7) // 8), LANES), jnp.int32),
            dma((seqs, pieces_of(hid_width))),
            dma((seqs,)),
            dma((2,)),
            dma((seqs,)),
            dma((seqs,)),
            dma((seqs,)),
            dma((seqs,)),
            dma((seqs,)),
            dma((seqs,)),
            dma((2,)),
            dma((2,)),
        ],
        compiler_params=pltpu.CompilerParams(
            collective_id=0, has_side_effects=True, vmem_limit_bytes=48 * 1024 * 1024
        ),
        cost_estimate=pl.CostEstimate(
            flops=flops,
            bytes_accessed=2 * (seqs * tokens + rank) * (hid_width + og_width),
            transcendentals=0,
        ),
    )(
        lengths,
        language,
        owner,
        owner.reshape(1, -1),
        left_inv,
        right_inv,
        hidden,
        out_grad,
        proj_in,
        proj_out,
    )


def solution(mesh):
    return jax.shard_map(
        per_device,
        mesh=mesh,
        in_specs=(
            P("dp", None, "tensor"),
            P("dp", None, "tensor"),
            P(None, "tensor"),
            P(None, "tensor"),
            P(),
            P(),
            P("dp"),
            P("dp"),
            P(),
        ),
        out_specs=(P("dp", "tensor"), P("dp", "tensor")),
        check_vma=False,
    )
```

time: 132 us -> 37.6 us (0.28)
  blocking collectives: 88.5 us -> 0 us
  Pallas kernels: 0 us -> 27.8 us
  between operations: 15.5 us -> 0.66 us
  matrix products: 12.5 us -> 0 us
  starting transfers between devices: 5.58 us -> 0 us
  local copies, waits for them, and re-layouts: 5.54 us -> 8.74 us
  other arithmetic: 2.31 us -> 0 us
    unnamed x2 -> x0, blocking collectives: 88.5 us -> none
    pallas_call x0 -> x1, Pallas kernels: none -> 27.8 us  [per_device(): pl.pallas_call(functools.partial(kernel, (t_size, outer, inner, slots)),...]
    dot_general x6 -> x0, matrix products: 12.5 us -> none  [the longest x2 9 us: project(): lax.dot_general(flattened, projection, (((1,), (1,)), ((), ())), preferre...]
    unnamed x2 -> x0, starting transfers between devices: 5.54 us -> none
    unnamed x21 -> x18, local copies, waits for them, and re-layouts: 3.21 us -> 8.74 us
    reshape x4 -> x0, local copies, waits for them, and re-layouts: 2.3 us -> none  [the longest x1 0.81 us: per_device(): right_full.reshape(seq_count, seq_length, proj_rank)]
  transfers between devices with their start and end apart: 3 -> 0, of which waited for: 1 -> 0; matrix products, arithmetic and copies ran while one was open for 1% -> 0% of each run, Pallas kernels for 0% -> 0%
where the time goes in v1:
time: 37.6 us; the launch traced here: 37.2 us
  Pallas kernels  27.8 us (74%)
  local copies, waits for them, and re-layouts  8.74 us (23%)
  between operations  0.66 us (2%)
    pallas_call x1, Pallas kernels, per_device(): pl.pallas_call(functools.partial(kernel, (t_size, outer, inner, slots)),...  27.8 us
    unnamed x18, local copies, waits for them, and re-layouts  8.74 us

profile of v1, /device:TPU:0, one launch (start us, length us, event | category | flops | bytes accessed | tf_op | source)
XLA Modules:
  0.0 37.2 jit_solution(11208212887103975694)
XLA Ops:
  0.6 0.0 copy-start
  0.6 1.9 %copy-done = bf16[3,256,2048]{2,1,0:T(8,128)(2,1)S(1)} copy-done((bf16[3,256,2048]{2,1,0:T(8,128)(2,1)S(1)}, bf16[3,256,2048]{2,1,0:T(8,128)(2,1)}, u32[]{:S(2)}) %copy-start) | copy-done | bytes 3145752
  2.5 0.0 copy-start.1
  2.5 1.2 %copy-done.1 = bf16[64,7168]{1,0:T(8,128)(2,1)S(1)} copy-done((bf16[64,7168]{1,0:T(8,128)(2,1)S(1)}, bf16[64,7168]{1,0:T(8,128)(2,1)}, u32[]{:S(2)}) %copy-start.1) | copy-done | bytes 917528
  3.7 0.0 copy-start.2
  3.7 0.9 %copy-done.2 = bf16[64,2048]{1,0:T(8,128)(2,1)S(1)} copy-done((bf16[64,2048]{1,0:T(8,128)(2,1)S(1)}, bf16[64,2048]{1,0:T(8,128)(2,1)}, u32[]{:S(2)}) %copy-start.2) | copy-done | bytes 262168
  4.7 0.0 copy-start.3
  4.7 0.8 %copy-done.3 = f32[64,64]{1,0:T(8,128)S(1)} copy-done((f32[64,64]{1,0:T(8,128)S(1)}, f32[64,64]{1,0:T(8,128)}, u32[]{:S(2)}) %copy-start.3) | copy-done | bytes 16408
  5.4 0.0 copy-start.4
  5.4 0.8 %copy-done.4 = f32[64,64]{1,0:T(8,128)S(1)} copy-done((f32[64,64]{1,0:T(8,128)S(1)}, f32[64,64]{1,0:T(8,128)}, u32[]{:S(2)}) %copy-start.4) | copy-done | bytes 16408
  6.2 0.0 copy-start.5
  6.2 0.7 %copy-done.5 = s32[100]{0:T(128)S(1)} copy-done((s32[100]{0:T(128)S(1)}, s32[100]{0:T(128)}, u32[]{:S(2)}) %copy-start.5) | copy-done | bytes 424
  6.8 0.0 copy-start.6
  6.8 0.7 %copy-done.6 = s32[3]{0:T(128)S(1)} copy-done((s32[3]{0:T(128)S(1)}, s32[3]{0:T(128)}, u32[]{:S(2)}) %copy-start.6) | copy-done | bytes 36
  7.5 0.0 copy-start.7
  7.5 0.7 %copy-done.7 = s32[3]{0:T(128)S(1)} copy-done((s32[3]{0:T(128)S(1)}, s32[3]{0:T(128)}, u32[]{:S(2)}) %copy-start.7) | copy-done | bytes 36
  8.1 27.8 %shard_map.104 = (f32[3,2048]{1,0:T(4,128)S(1)}, f32[7,2048]{1,0:T(8,128)S(1)}) custom-call(s32[3]{0:T(128)S(1)} %copy-done.6, s32[3]{0:T(128)S(1)} %copy-done.7, s32[100]{0:T(128)S(1)} %copy-done.5, s32[1,100]{1,0:T(1,128)S(1)} %bitcast.1, f32[64,64]{1,0:T(8,128)S(1)} %copy-done.3, f32[64,64]{1,0:T(8,128)S(1)} %copy-done.4, bf16[3,256,7168]{2,1,0:T(8,128)(2,1)} %hidden.1, ...), custom_call_target="tpu_custom_call" | custom-call | flops 905969664 | bytes 15335424 | tf_op jit(solution)/shard_map/pallas_call | solution.py:280
  36.0 0.6 %copy.13 = f32[3,2048]{1,0:T(4,128)} copy(f32[3,2048]{1,0:T(4,128)S(1)} %get-tuple-element.4) | data formatting | bytes 49152
  36.6 0.6 %copy.14 = f32[7,2048]{1,0:T(8,128)} copy(f32[7,2048]{1,0:T(8,128)S(1)} %get-tuple-element.5) | data formatting | bytes 114688
Async XLA Ops:
  0.6 1.9 %copy-start = (bf16[3,256,2048]{2,1,0:T(8,128)(2,1)S(1)}, bf16[3,256,2048]{2,1,0:T(8,128)(2,1)}, u32[]{:S(2)}) copy-start(bf16[3,256,2048]{2,1,0:T(8,128)(2,1)} %out_grad.1) | copy-start | bytes 9437188
  2.5 1.2 %copy-start.1 = (bf16[64,7168]{1,0:T(8,128)(2,1)S(1)}, bf16[64,7168]{1,0:T(8,128)(2,1)}, u32[]{:S(2)}) copy-start(bf16[64,7168]{1,0:T(8,128)(2,1)} %proj_in.1) | copy-start | bytes 2752516
  3.7 0.9 %copy-start.2 = (bf16[64,2048]{1,0:T(8,128)(2,1)S(1)}, bf16[64,2048]{1,0:T(8,128)(2,1)}, u32[]{:S(2)}) copy-start(bf16[64,2048]{1,0:T(8,128)(2,1)} %proj_out.1) | copy-start | bytes 786436
  4.7 0.8 %copy-start.3 = (f32[64,64]{1,0:T(8,128)S(1)}, f32[64,64]{1,0:T(8,128)}, u32[]{:S(2)}) copy-start(f32[64,64]{1,0:T(8,128)} %left_inv.1) | copy-start | bytes 49156
  5.4 0.8 %copy-start.4 = (f32[64,64]{1,0:T(8,128)S(1)}, f32[64,64]{1,0:T(8,128)}, u32[]{:S(2)}) copy-start(f32[64,64]{1,0:T(8,128)} %right_inv.1) | copy-start | bytes 49156
  6.2 0.7 %copy-start.5 = (s32[100]{0:T(128)S(1)}, s32[100]{0:T(128)}, u32[]{:S(2)}) copy-start(s32[100]{0:T(128)} %owner_list.1) | copy-start | bytes 1204
  6.8 0.7 %copy-start.6 = (s32[3]{0:T(128)S(1)}, s32[3]{0:T(128)}, u32[]{:S(2)}) copy-start(s32[3]{0:T(128)} %lengths.1) | copy-start | bytes 40
  7.5 0.7 %copy-start.7 = (s32[3]{0:T(128)S(1)}, s32[3]{0:T(128)}, u32[]{:S(2)}) copy-start(s32[3]{0:T(128)} %language.1) | copy-start | bytes 40

commit v2 on v1

--- a/solution.py
+++ b/solution.py
@@ -21,12 +21,12 @@
 
 def kernel(
     sizes,
-    lengths,
-    language,
-    owner_list,
-    owner_row,
-    left_inv,
-    right_inv,
+    lengths_in,
+    language_in,
+    owner_in,
+    owner_row_in,
+    left_inv_in,
+    right_inv_in,
     hidden,
     out_grad,
     proj_in,
@@ -40,11 +40,21 @@
     part,
     peer_part,
     g_scr,
+    pairs,
     gathered,
     places,
+    sums,
+    counts,
+    lengths,
+    language,
+    owner_list,
+    owner_row,
+    left_inv,
+    right_inv,
     hid_sem,
     og_sem,
     w_sem,
+    small_sem,
     t_send,
     t_recv,
     z_send,
@@ -59,6 +69,7 @@
     rank = w_in.shape[0]
     half = rank // t_size
     rows = half // 2
+    wide = 2 * rank
     dp = lax.axis_index("dp")
     t_me = lax.axis_index("tensor")
     my_out = dp // inner
@@ -66,24 +77,51 @@
     hid_pieces = pieces_of(hid_width)
     piece = hid_width // hid_pieces
 
+    def og_copy(s):
+        return pltpu.make_async_copy(out_grad.at[s], og.at[s], og_sem.at[s])
+
+    def hid_copy(s, c):
+        cols = pl.ds(pl.multiple_of(c * piece, LANES), piece)
+        return pltpu.make_async_copy(
+            hidden.at[s, :, cols], hid.at[s, :, cols], hid_sem.at[s, c]
+        )
+
     w_in_copy = pltpu.make_async_copy(proj_in, w_in, w_sem.at[0])
     w_out_copy = pltpu.make_async_copy(proj_out, w_out, w_sem.at[1])
+    small_copies = [
+        pltpu.make_async_copy(source, target, small_sem.at[n])
+        for n, (source, target) in enumerate(
+            (
+                (language_in, language),
+                (owner_in, owner_list),
+                (owner_row_in, owner_row),
+                (lengths_in, lengths),
+                (left_inv_in, left_inv),
+                (right_inv_in, right_inv),
+            )
+        )
+    ]
     w_out_copy.start()
-    og_copies = []
-    hid_copies = []
-    for s in range(seqs):
-        og_copies.append(pltpu.make_async_copy(out_grad.at[s], og.at[s], og_sem.at[s]))
-        og_copies[s].start()
-        if s == 0:
-            w_in_copy.start()
-        for c in range(hid_pieces):
-            cols = pl.ds(c * piece, piece)
-            hid_copies.append(
-                pltpu.make_async_copy(
-                    hidden.at[s, :, cols], hid.at[s, :, cols], hid_sem.at[s, c]
-                )
-            )
-            hid_copies[-1].start()
+    og_copy(0).start()
+    w_in_copy.start()
+    for copy in small_copies:
+        copy.start()
+
+    def start_sequence(s):
+        def start_piece(c, carry):
+            hid_copy(s, c).start()
+            return carry
+
+        lax.fori_loop(0, hid_pieces, start_piece, None)
+
+    start_sequence(0)
+
+    def start_later(s, carry):
+        og_copy(s).start()
+        start_sequence(s)
+        return carry
+
+    lax.fori_loop(1, seqs, start_later, None)
 
     def t_peer(k):
         return (dp, (t_me + k) % t_size)
@@ -102,6 +140,8 @@
                 barrier, inc=1, device_id=peer_of(k), device_id_type=pl.DeviceIdType.MESH
             )
 
+    for copy in small_copies:
+        copy.wait()
     own_row = owner_row[...]
     lang_lane = lax.broadcasted_iota(jnp.int32, own_row.shape, 1)
     sub = lax.broadcasted_iota(jnp.int32, places.shape[2:], 0)
@@ -113,6 +153,8 @@
         slot = jnp.sum(earlier.astype(jnp.int32), axis=1, keepdims=True)
         place_block = jnp.where(sub == s, own * slots + slot, place_block)
     places[my_in, my_out] = place_block
+    sums[...] = jnp.zeros_like(sums)
+    counts[...] = jnp.zeros_like(counts)
 
     def send(src, dst, send_sem, recv_sem, peer):
         pltpu.make_async_remote_copy(
@@ -128,21 +170,19 @@
         pltpu.make_async_copy(block, block, sem).wait()
 
     def project(s):
-        og_copies[s].wait()
+        og_copy(s).wait()
         dims = (((1,), (1,)), ((), ()))
         right = lax.dot_general(og[s], w_out[...], dims, preferred_element_type=jnp.float32)
-        left = jnp.zeros((tokens, rank), jnp.float32)
-        for c in range(hid_pieces):
-            if s == 0 and c == 0:
-                w_in_copy.wait()
-            hid_copies[s * hid_pieces + c].wait()
-            cols = slice(c * piece, (c + 1) * piece)
-            left += lax.dot_general(
+
+        def add_piece(c, left):
+            hid_copy(s, c).wait()
+            cols = pl.ds(pl.multiple_of(c * piece, LANES), piece)
+            return left + lax.dot_general(
                 hid[s, :, cols], w_in[:, cols], dims, preferred_element_type=jnp.float32
             )
+
+        left = lax.fori_loop(0, hid_pieces, add_piece, jnp.zeros((tokens, rank), jnp.float32))
         part[s] = jnp.concatenate([left, right], axis=1)
-
-    def send_part(s):
         for k in range(1, t_size):
             send(part.at[s], peer_part.at[s, k - 1], t_send.at[s], t_recv.at[s], t_peer(k))
 
@@ -164,11 +204,10 @@
         full = lax.dot_general(
             split, split, (((0,), (0,)), ((), ())), preferred_element_type=jnp.float32
         )
-        wide = 2 * rank
         full = full[0:rank] + full[wide : wide + rank]
         full = full[:, 0:wide] + full[:, wide : 2 * wide]
         grads = full[:, rank:wide]
-        g_scr[s] = grads
+        g_scr[...] = grads
         left_rows = jnp.concatenate([left_inv[even, :], left_inv[odd, :]], axis=0)
         done = jnp.dot(left_rows, grads, precision=HIGHEST, preferred_element_type=jnp.float32)
         pre = jnp.dot(
@@ -178,71 +217,92 @@
         for k in range(1, outer):
             block = gathered.at[s, my_in, my_out]
             send(block, block, z_send.at[s], z_recv.at[s], z_peer(k))
-        pair = jnp.concatenate([g_scr[s, even, :], g_scr[s, odd, :]], axis=1)
-        for r in range(rows):
-            grads_out[s : s + 1, r * LANES : (r + 1) * LANES] = pair[r : r + 1]
+        pairs[s] = jnp.concatenate([g_scr[even, :], g_scr[odd, :]], axis=1)
 
     def forward(s):
-        if s == 0:
+        @pl.when(s == 0)
+        def _():
             if outer > 1:
                 take(places.at[0, pl.ds(0, outer - 1)], m_recv.at[0])
             for k in range(1, inner):
                 block = places.at[my_in]
                 send(block, block, m_send.at[1], m_recv.at[1], p_peer(k))
+
         if outer > 1:
             take(gathered.at[s, 0, pl.ds(0, outer - 1)], z_recv.at[s])
         for k in range(1, inner):
             block = gathered.at[s, my_in]
             send(block, block, p_send.at[s], p_recv.at[s], p_peer(k))
 
-    def accumulate(s, held):
-        if s == 0 and inner > 1:
-            take(places.at[pl.ds(0, inner - 1)], m_recv.at[1])
+    def accumulate(s):
         if inner > 1:
+
+            @pl.when(s == 0)
+            def _():
+                take(places.at[pl.ds(0, inner - 1)], m_recv.at[1])
+
             take(gathered.at[s, pl.ds(0, inner - 1)], p_recv.at[s])
 
-        def step(i, held):
-            sums, counts = held
-            sums, counts = list(sums), list(counts)
+        def add_block(i, held):
+            total, seen = list(held[0]), list(held[1])
             for o in range(outer):
-                place = places[i, o, s : s + 1, :]
+                place = places[i, o, pl.ds(s, 1), :]
                 row = gathered[s, i, o]
                 for j in range(slots):
                     hit = (place == dp * slots + j).astype(jnp.float32)
-                    sums[j] = sums[j] + hit * row
-                    counts[j] = counts[j] + hit
-            return tuple(sums), tuple(counts)
-
-        return lax.fori_loop(0, inner, step, held)
+                    total[j] = total[j] + hit * row
+                    seen[j] = seen[j] + hit
+            return tuple(total), tuple(seen)
+
+        total, seen = lax.fori_loop(
+            0,
+            inner,
+            add_block,
+            (
+                tuple(sums[j] for j in range(slots)),
+                tuple(counts[pl.ds(j, 1), :] for j in range(slots)),
+            ),
+        )
+        for j in range(slots):
+            sums[j] = total[j]
+            counts[pl.ds(j, 1), :] = seen[j]
 
     w_out_copy.wait()
-    for s in range(seqs):
-        project(s)
-        if s == 0:
-            pl.semaphore_wait(barrier, sum(count - 1 for _, count in peers))
-            for k in range(1, outer):
-                block = places.at[my_in, my_out]
-                send(block, block, m_send.at[0], m_recv.at[0], z_peer(k))
-        send_part(s)
-        if s >= 2:
-            forward(s - 2)
-        if s >= 1:
-            reduce(s - 1)
-    if seqs >= 2:
-        forward(seqs - 2)
-    reduce(seqs - 1)
-    held = (
-        tuple(jnp.zeros((rows, LANES), jnp.float32) for _ in range(slots)),
-        tuple(jnp.zeros((1, LANES), jnp.float32) for _ in range(slots)),
-    )
-    for s in range(seqs - 2):
-        held = accumulate(s, held)
-    forward(seqs - 1)
-    for s in range(max(seqs - 2, 0), seqs):
-        held = accumulate(s, held)
-    sums, counts = held
+    w_in_copy.wait()
+    pl.semaphore_wait(barrier, sum(count - 1 for _, count in peers))
+    for k in range(1, outer):
+        block = places.at[my_in, my_out]
+        send(block, block, m_send.at[0], m_recv.at[0], z_peer(k))
+
+    def step(i, carry):
+        @pl.when(i < seqs)
+        def _():
+            project(i)
+
+        @pl.when((i >= 1) & (i <= seqs))
+        def _():
+            reduce(i - 1)
+
+        @pl.when((i >= 2) & (i <= seqs + 1))
+        def _():
+            forward(i - 2)
+
+        @pl.when(i == seqs + 1)
+        def _():
+            for s in range(seqs):
+                pair = pairs[s]
+                for r in range(rows):
+                    grads_out[s : s + 1, r * LANES : (r + 1) * LANES] = pair[r : r + 1]
+
+        @pl.when(i >= 3)
+        def _():
+            accumulate(i - 3)
+
+        return carry
+
+    lax.fori_loop(0, seqs + 3, step, None)
     for j in range(slots):
-        mean = sums[j] / jnp.maximum(counts[j], 1.0)
+        mean = sums[j] / jnp.maximum(counts[pl.ds(j, 1), :], 1.0)
         for r in range(rows):
             means_out[j : j + 1, r * LANES : (r + 1) * LANES] = mean[r : r + 1]
 
@@ -272,7 +332,6 @@
     slots = (owner.shape[0] + dp_size - 1) // dp_size
     half = rank // t_size
     rows = half * rank // LANES
-    smem = pl.BlockSpec(memory_space=pltpu.SMEM)
     vmem = pl.BlockSpec(memory_space=pltpu.VMEM)
     anywhere = pl.BlockSpec(memory_space=pl.ANY)
     dma = pltpu.SemaphoreType.DMA
@@ -283,7 +342,7 @@
             jax.ShapeDtypeStruct((seqs, half * rank), jnp.float32),
             jax.ShapeDtypeStruct((slots, half * rank), jnp.float32),
         ),
-        in_specs=[smem, smem, smem, vmem, vmem, vmem] + [anywhere] * 4,
+        in_specs=[anywhere] * 10,
         out_specs=(vmem, vmem),
         scratch_shapes=[
             pltpu.VMEM((seqs, tokens, hid_width), jnp.bfloat16),
@@ -292,12 +351,22 @@
             pltpu.VMEM((rank, og_width), jnp.bfloat16),
             pltpu.VMEM((seqs, tokens, 2 * rank), jnp.float32),
             pltpu.VMEM((seqs, max(t_size - 1, 1), tokens, 2 * rank), jnp.float32),
-            pltpu.VMEM((seqs, rank, rank), jnp.float32),
+            pltpu.VMEM((rank, rank), jnp.float32),
+            pltpu.VMEM((seqs, rows, LANES), jnp.float32),
             pltpu.VMEM((seqs, inner, outer, rows, LANES), jnp.float32),
             pltpu.VMEM((inner, outer, 8 * ((seqs + 7) // 8), LANES), jnp.int32),
+            pltpu.VMEM((slots, rows, LANES), jnp.float32),
+            pltpu.VMEM((8 * ((slots + 7) // 8), LANES), jnp.float32),
+            pltpu.SMEM((seqs,), jnp.int32),
+            pltpu.SMEM((seqs,), jnp.int32),
+            pltpu.SMEM(owner.shape, jnp.int32),
+            pltpu.VMEM((1, owner.shape[0]), jnp.int32),
+            pltpu.VMEM((rank, rank), jnp.float32),
+            pltpu.VMEM((rank, rank), jnp.float32),
             dma((seqs, pieces_of(hid_width))),
             dma((seqs,)),
             dma((2,)),
+            dma((6,)),
             dma((seqs,)),
             dma((seqs,)),
             dma((seqs,)),
@@ -308,7 +377,7 @@
             dma((2,)),
         ],
         compiler_params=pltpu.CompilerParams(
-            collective_id=0, has_side_effects=True, vmem_limit_bytes=48 * 1024 * 1024
+            collective_id=0, has_side_effects=True, vmem_limit_bytes=64 * 1024 * 1024
         ),
         cost_estimate=pl.CostEstimate(
             flops=flops,

time: 37.6 us -> 27.4 us (0.73)
  local copies, waits for them, and re-layouts: 8.74 us -> 2.85 us
  Pallas kernels: 27.8 us -> 23.7 us
    unnamed x18 -> x2, local copies, waits for them, and re-layouts: 8.74 us -> 2.85 us
    pallas_call x1, Pallas kernels: 27.8 us -> 23.7 us  [per_device(): pl.pallas_call(functools.partial(kernel, (t_size, outer, inner, slots)),...]
where the time goes in v2:
time: 27.4 us; the launch traced here: 27.2 us
  Pallas kernels  23.7 us (86%)
  local copies, waits for them, and re-layouts  2.85 us (10%)
  between operations  0.64 us (2%)
    pallas_call x1, Pallas kernels, per_device(): pl.pallas_call(functools.partial(kernel, (t_size, outer, inner, slots)),...  23.7 us
    unnamed x2, local copies, waits for them, and re-layouts  2.85 us

profile of v2, /device:TPU:0, one launch (start us, length us, event | category | flops | bytes accessed | tf_op | source)
XLA Modules:
  0.0 27.2 jit_solution(7180202256643400227)
XLA Ops:
  0.6 23.7 %shard_map.104 = (f32[3,2048]{1,0:T(4,128)}, f32[7,2048]{1,0:T(8,128)}) custom-call(s32[3]{0:T(128)} %lengths_in.1, s32[3]{0:T(128)} %language_in.1, s32[100]{0:T(128)} %owner_in.1, s32[1,100]{1,0:T(1,128)} %bitcast.1, f32[64,64]{1,0:T(8,128)} %left_inv_in.1, f32[64,64]{1,0:T(8,128)} %right_inv_in.1, bf16[3,256,7168]{2,1,0:T(8,128)(2,1)} %hidden.1, ...), custom_call_target="tpu_custom_call" | custom-call | flops 905969664 | bytes 15335424 | tf_op jit(solution)/shard_map/pallas_call | solution.py:339
  24.4 1.4 %copy.13 = f32[3,2048]{1,0:T(4,128)} copy(f32[3,2048]{1,0:T(4,128)} %get-tuple-element.4) | data formatting | bytes 49152
  25.7 1.5 %copy.14 = f32[7,2048]{1,0:T(8,128)} copy(f32[7,2048]{1,0:T(8,128)} %get-tuple-element.5) | data formatting | bytes 114688

commit v3 on v2

--- a/solution.py
+++ b/solution.py
@@ -9,7 +9,6 @@
 from jax.sharding import PartitionSpec as P
 
 LANES = 128
-HIGHEST = lax.Precision.HIGHEST
 
 
 def pieces_of(width):
@@ -17,6 +16,23 @@
         if width % (count * 256) == 0:
             return count
     return 1
+
+
+def halves(values):
+    high = values.astype(jnp.bfloat16)
+    return high, (values - high.astype(jnp.float32)).astype(jnp.bfloat16)
+
+
+def finish(slots, rows_in, grads_out, means_out):
+    rows = rows_in.shape[1]
+    for n in range(rows_in.shape[0]):
+        block = rows_in[n]
+        for r in range(rows):
+            cols = slice(r * LANES, (r + 1) * LANES)
+            if n < slots:
+                means_out[n : n + 1, cols] = block[r : r + 1]
+            else:
+                grads_out[n - slots : n - slots + 1, cols] = block[r : r + 1]
 
 
 def kernel(
@@ -31,8 +47,7 @@
     out_grad,
     proj_in,
     proj_out,
-    grads_out,
-    means_out,
+    out,
     hid,
     og,
     w_in,
@@ -40,7 +55,8 @@
     part,
     peer_part,
     g_scr,
-    pairs,
+    l_split,
+    r_split,
     gathered,
     places,
     sums,
@@ -169,10 +185,10 @@
     def take(block, sem):
         pltpu.make_async_copy(block, block, sem).wait()
 
-    def project(s):
-        og_copy(s).wait()
+    early = (hid_pieces + 1) // 2
+
+    def project(s, begin, end):
         dims = (((1,), (1,)), ((), ()))
-        right = lax.dot_general(og[s], w_out[...], dims, preferred_element_type=jnp.float32)
 
         def add_piece(c, left):
             hid_copy(s, c).wait()
@@ -181,10 +197,17 @@
                 hid[s, :, cols], w_in[:, cols], dims, preferred_element_type=jnp.float32
             )
 
-        left = lax.fori_loop(0, hid_pieces, add_piece, jnp.zeros((tokens, rank), jnp.float32))
-        part[s] = jnp.concatenate([left, right], axis=1)
-        for k in range(1, t_size):
-            send(part.at[s], peer_part.at[s, k - 1], t_send.at[s], t_recv.at[s], t_peer(k))
+        if begin == 0:
+            og_copy(s).wait()
+            left = jnp.zeros((tokens, rank), jnp.float32)
+            right = lax.dot_general(og[s], w_out[...], dims, preferred_element_type=jnp.float32)
+            part[s, :, rank:wide] = right
+        else:
+            left = part[s, :, 0:rank]
+        part[s, :, 0:rank] = lax.fori_loop(begin, end, add_piece, left)
+        if end == hid_pieces:
+            for k in range(1, t_size):
+                send(part.at[s], peer_part.at[s, k - 1], t_send.at[s], t_recv.at[s], t_peer(k))
 
     first = t_me * half
     even = pl.ds(first, rows, stride=2)
@@ -198,8 +221,7 @@
             both += peer_part[s, k - 1]
         token = lax.broadcasted_iota(jnp.int32, both.shape, 0)
         both = jnp.where(token < lengths[s], both, 0.0)
-        high = both.astype(jnp.bfloat16)
-        low = (both - high.astype(jnp.float32)).astype(jnp.bfloat16)
+        high, low = halves(both)
         split = jnp.concatenate([high, low], axis=1)
         full = lax.dot_general(
             split, split, (((0,), (0,)), ((), ())), preferred_element_type=jnp.float32
@@ -208,16 +230,23 @@
         full = full[:, 0:wide] + full[:, wide : 2 * wide]
         grads = full[:, rank:wide]
         g_scr[...] = grads
-        left_rows = jnp.concatenate([left_inv[even, :], left_inv[odd, :]], axis=0)
-        done = jnp.dot(left_rows, grads, precision=HIGHEST, preferred_element_type=jnp.float32)
+        high, low = halves(grads)
+        done = jnp.dot(
+            l_split[...],
+            jnp.concatenate([high, low, high], axis=0),
+            preferred_element_type=jnp.float32,
+        )
+        high, low = halves(done)
         pre = jnp.dot(
-            done, right_inv[...], precision=HIGHEST, preferred_element_type=jnp.float32
+            jnp.concatenate([high, low, high], axis=1),
+            r_split[...],
+            preferred_element_type=jnp.float32,
         )
         gathered[s, my_in, my_out] = jnp.concatenate([pre[:rows], pre[rows:]], axis=1)
         for k in range(1, outer):
             block = gathered.at[s, my_in, my_out]
             send(block, block, z_send.at[s], z_recv.at[s], z_peer(k))
-        pairs[s] = jnp.concatenate([g_scr[even, :], g_scr[odd, :]], axis=1)
+        out[slots + s] = jnp.concatenate([g_scr[even, :], g_scr[odd, :]], axis=1)
 
     def forward(s):
         @pl.when(s == 0)
@@ -274,37 +303,40 @@
         block = places.at[my_in, my_out]
         send(block, block, m_send.at[0], m_recv.at[0], z_peer(k))
 
+    left_rows = jnp.concatenate([left_inv[even, :], left_inv[odd, :]], axis=0)
+    high, low = halves(left_rows)
+    l_split[...] = jnp.concatenate([high, high, low], axis=1)
+    high, low = halves(right_inv[...])
+    r_split[...] = jnp.concatenate([high, high, low], axis=0)
+
     def step(i, carry):
         @pl.when(i < seqs)
         def _():
-            project(i)
+            project(i, 0, early)
 
         @pl.when((i >= 1) & (i <= seqs))
         def _():
             reduce(i - 1)
 
-        @pl.when((i >= 2) & (i <= seqs + 1))
+        if early < hid_pieces:
+
+            @pl.when(i < seqs)
+            def _():
+                project(i, early, hid_pieces)
+
+        @pl.when((i >= 1) & (i <= seqs))
         def _():
-            forward(i - 2)
-
-        @pl.when(i == seqs + 1)
+            forward(i - 1)
+
+        @pl.when(i >= 2)
         def _():
-            for s in range(seqs):
-                pair = pairs[s]
-                for r in range(rows):
-                    grads_out[s : s + 1, r * LANES : (r + 1) * LANES] = pair[r : r + 1]
-
-        @pl.when(i >= 3)
-        def _():
-            accumulate(i - 3)
+            accumulate(i - 2)
 
         return carry
 
-    lax.fori_loop(0, seqs + 3, step, None)
+    lax.fori_loop(0, seqs + 2, step, None)
     for j in range(slots):
-        mean = sums[j] / jnp.maximum(counts[pl.ds(j, 1), :], 1.0)
-        for r in range(rows):
-            means_out[j : j + 1, r * LANES : (r + 1) * LANES] = mean[r : r + 1]
+        out[j] = sums[j] / jnp.maximum(counts[pl.ds(j, 1), :], 1.0)
 
     for s in range(seqs):
         if t_size > 1:
@@ -336,14 +368,11 @@
     anywhere = pl.BlockSpec(memory_space=pl.ANY)
     dma = pltpu.SemaphoreType.DMA
     flops = 2 * seqs * tokens * rank * (hid_width + og_width)
-    return pl.pallas_call(
+    blocks = pl.pallas_call(
         functools.partial(kernel, (t_size, outer, inner, slots)),
-        out_shape=(
-            jax.ShapeDtypeStruct((seqs, half * rank), jnp.float32),
-            jax.ShapeDtypeStruct((slots, half * rank), jnp.float32),
-        ),
+        out_shape=jax.ShapeDtypeStruct((slots + seqs, rows, LANES), jnp.float32),
         in_specs=[anywhere] * 10,
-        out_specs=(vmem, vmem),
+        out_specs=vmem,
         scratch_shapes=[
             pltpu.VMEM((seqs, tokens, hid_width), jnp.bfloat16),
             pltpu.VMEM((seqs, tokens, og_width), jnp.bfloat16),
@@ -352,7 +381,8 @@
             pltpu.VMEM((seqs, tokens, 2 * rank), jnp.float32),
             pltpu.VMEM((seqs, max(t_size - 1, 1), tokens, 2 * rank), jnp.float32),
             pltpu.VMEM((rank, rank), jnp.float32),
-            pltpu.VMEM((seqs, rows, LANES), jnp.float32),
+            pltpu.VMEM((half, 3 * rank), jnp.bfloat16),
+            pltpu.VMEM((3 * rank, rank), jnp.bfloat16),
             pltpu.VMEM((seqs, inner, outer, rows, LANES), jnp.float32),
             pltpu.VMEM((inner, outer, 8 * ((seqs + 7) // 8), LANES), jnp.int32),
             pltpu.VMEM((slots, rows, LANES), jnp.float32),
@@ -396,6 +426,15 @@
         proj_in,
         proj_out,
     )
+    return pl.pallas_call(
+        functools.partial(finish, slots),
+        out_shape=(
+            jax.ShapeDtypeStruct((seqs, half * rank), jnp.float32),
+            jax.ShapeDtypeStruct((slots, half * rank), jnp.float32),
+        ),
+        in_specs=[vmem],
+        out_specs=(vmem, vmem),
+    )(blocks)
 
 
 def solution(mesh):

time: 27.4 us -> 30.5 us (1.11)
  Pallas kernels: 23.7 us -> 29.7 us
  local copies, waits for them, and re-layouts: 2.85 us -> 0 us
    pallas_call x1, Pallas kernels: 23.7 us -> 28.1 us  [per_device(): pl.pallas_call(functools.partial(kernel, (t_size, outer, inner, slots)),...]
    unnamed x2 -> x0, local copies, waits for them, and re-layouts: 2.85 us -> none
    pallas_call x0 -> x1, Pallas kernels: none -> 1.56 us  [per_device(): pl.pallas_call(functools.partial(finish, slots), out_shape=(jax.ShapeDtyp...]
where the time goes in v3:
time: 30.5 us; the launch traced here: 30.3 us
  Pallas kernels  29.7 us (97%)
  between operations  0.64 us (2%)
    pallas_call x1, Pallas kernels, per_device(): pl.pallas_call(functools.partial(kernel, (t_size, outer, inner, slots)),...  28.1 us
    pallas_call x1, Pallas kernels, per_device(): pl.pallas_call(functools.partial(finish, slots), out_shape=(jax.ShapeDtyp...  1.56 us

profile of v3, /device:TPU:0, one launch (start us, length us, event | category | flops | bytes accessed | tf_op | source)
XLA Modules:
  0.0 30.3 jit_solution(7193795782789474906)
XLA Ops:
  0.6 28.1 %shard_map.104.rows_in = f32[10,16,128]{2,1,0:T(8,128)} custom-call(s32[3]{0:T(128)} %lengths_in.1, s32[3]{0:T(128)} %language_in.1, s32[100]{0:T(128)} %owner_in.1, s32[1,100]{1,0:T(1,128)} %bitcast.1, f32[64,64]{1,0:T(8,128)} %left_inv_in.1, f32[64,64]{1,0:T(8,128)} %right_inv_in.1, bf16[3,256,7168]{2,1,0:T(8,128)(2,1)} %hidden.1, ...), custom_call_target="tpu_custom_call" | custom-call | flops 905969664 | bytes 15335424 | tf_op jit(solution)/shard_map/pallas_call | solution.py:371
  28.8 1.6 %shard_map.105 = (f32[3,2048]{1,0:T(4,128)}, f32[7,2048]{1,0:T(8,128)}) custom-call(f32[10,16,128]{2,1,0:T(8,128)} %shard_map.104.rows_in), custom_call_target="tpu_custom_call" | custom-call | tf_op jit(solution)/shard_map/pallas_call | solution.py:429

commit v4 on v3

--- a/solution.py
+++ b/solution.py
@@ -92,6 +92,7 @@
     my_in = dp % inner
     hid_pieces = pieces_of(hid_width)
     piece = hid_width // hid_pieces
+    cut = 256 * ((piece // 256 + 1) // 2)
 
     def og_copy(s):
         return pltpu.make_async_copy(out_grad.at[s], og.at[s], og_sem.at[s])
@@ -123,21 +124,11 @@
     for copy in small_copies:
         copy.start()
 
-    def start_sequence(s):
-        def start_piece(c, carry):
-            hid_copy(s, c).start()
-            return carry
-
-        lax.fori_loop(0, hid_pieces, start_piece, None)
-
-    start_sequence(0)
-
-    def start_later(s, carry):
-        og_copy(s).start()
-        start_sequence(s)
+    def start_piece(c, carry):
+        hid_copy(0, c).start()
         return carry
 
-    lax.fori_loop(1, seqs, start_later, None)
+    lax.fori_loop(0, hid_pieces, start_piece, None)
 
     def t_peer(k):
         return (dp, (t_me + k) % t_size)
@@ -185,29 +176,37 @@
     def take(block, sem):
         pltpu.make_async_copy(block, block, sem).wait()
 
-    early = (hid_pieces + 1) // 2
-
-    def project(s, begin, end):
+    def project(s):
         dims = (((1,), (1,)), ((), ()))
+        og_copy(s).wait()
+
+        @pl.when(s + 1 < seqs)
+        def _():
+            og_copy(s + 1).start()
+
+        right = lax.dot_general(og[s], w_out[...], dims, preferred_element_type=jnp.float32)
+        part[s, :, rank:wide] = right
 
         def add_piece(c, left):
             hid_copy(s, c).wait()
-            cols = pl.ds(pl.multiple_of(c * piece, LANES), piece)
-            return left + lax.dot_general(
-                hid[s, :, cols], w_in[:, cols], dims, preferred_element_type=jnp.float32
-            )
-
-        if begin == 0:
-            og_copy(s).wait()
-            left = jnp.zeros((tokens, rank), jnp.float32)
-            right = lax.dot_general(og[s], w_out[...], dims, preferred_element_type=jnp.float32)
-            part[s, :, rank:wide] = right
-        else:
-            left = part[s, :, 0:rank]
-        part[s, :, 0:rank] = lax.fori_loop(begin, end, add_piece, left)
-        if end == hid_pieces:
-            for k in range(1, t_size):
-                send(part.at[s], peer_part.at[s, k - 1], t_send.at[s], t_recv.at[s], t_peer(k))
+
+            @pl.when(s + 1 < seqs)
+            def _():
+                hid_copy(s + 1, c).start()
+
+            base = pl.multiple_of(c * piece, LANES)
+            for begin, end in ((0, cut), (cut, piece)):
+                cols = pl.ds(base + begin, end - begin)
+                left += lax.dot_general(
+                    hid[s, :, cols], w_in[:, cols], dims, preferred_element_type=jnp.float32
+                )
+            return left
+
+        part[s, :, 0:rank] = lax.fori_loop(
+            0, hid_pieces, add_piece, jnp.zeros((tokens, rank), jnp.float32)
+        )
+        for k in range(1, t_size):
+            send(part.at[s], peer_part.at[s, k - 1], t_send.at[s], t_recv.at[s], t_peer(k))
 
     first = t_me * half
     even = pl.ds(first, rows, stride=2)
@@ -312,29 +311,23 @@
     def step(i, carry):
         @pl.when(i < seqs)
         def _():
-            project(i, 0, early)
+            project(i)
 
         @pl.when((i >= 1) & (i <= seqs))
         def _():
             reduce(i - 1)
 
-        if early < hid_pieces:
-
-            @pl.when(i < seqs)
-            def _():
-                project(i, early, hid_pieces)
-
-        @pl.when((i >= 1) & (i <= seqs))
-        def _():
-            forward(i - 1)
-
-        @pl.when(i >= 2)
-        def _():
-            accumulate(i - 2)
+        @pl.when((i >= 2) & (i <= seqs + 1))
+        def _():
+            forward(i - 2)
+
+        @pl.when(i >= 3)
+        def _():
+            accumulate(i - 3)
 
         return carry
 
-    lax.fori_loop(0, seqs + 2, step, None)
+    lax.fori_loop(0, seqs + 3, step, None)
     for j in range(slots):
         out[j] = sums[j] / jnp.maximum(counts[pl.ds(j, 1), :], 1.0)
 

time: 30.5 us -> 25.9 us (0.85)
  Pallas kernels: 29.7 us -> 25.1 us
    pallas_call x1, Pallas kernels: 28.1 us -> 23.6 us  [per_device(): pl.pallas_call(functools.partial(kernel, (t_size, outer, inner, slots)),...]
where the time goes in v4:
time: 25.9 us; the launch traced here: 25.8 us
  Pallas kernels  25.1 us (97%)
  between operations  0.64 us (2%)
    pallas_call x1, Pallas kernels, per_device(): pl.pallas_call(functools.partial(kernel, (t_size, outer, inner, slots)),...  23.6 us
    pallas_call x1, Pallas kernels, per_device(): pl.pallas_call(functools.partial(finish, slots), out_shape=(jax.ShapeDtyp...  1.56 us

profile of v4, /device:TPU:0, one launch (start us, length us, event | category | flops | bytes accessed | tf_op | source)
XLA Modules:
  0.0 25.8 jit_solution(7072675827989792294)
XLA Ops:
  0.6 23.6 %shard_map.104.rows_in = f32[10,16,128]{2,1,0:T(8,128)} custom-call(s32[3]{0:T(128)} %lengths_in.1, s32[3]{0:T(128)} %language_in.1, s32[100]{0:T(128)} %owner_in.1, s32[1,100]{1,0:T(1,128)} %bitcast.1, f32[64,64]{1,0:T(8,128)} %left_inv_in.1, f32[64,64]{1,0:T(8,128)} %right_inv_in.1, bf16[3,256,7168]{2,1,0:T(8,128)(2,1)} %hidden.1, ...), custom_call_target="tpu_custom_call" | custom-call | flops 905969664 | bytes 15335424 | tf_op jit(solution)/shard_map/pallas_call | solution.py:364
  24.2 1.6 %shard_map.105 = (f32[3,2048]{1,0:T(4,128)}, f32[7,2048]{1,0:T(8,128)}) custom-call(f32[10,16,128]{2,1,0:T(8,128)} %shard_map.104.rows_in), custom_call_target="tpu_custom_call" | custom-call | tf_op jit(solution)/shard_map/pallas_call | solution.py:422

commit v5 on v4

--- a/solution.py
+++ b/solution.py
@@ -77,6 +77,8 @@
     z_recv,
     p_send,
     p_recv,
+    d_send,
+    d_recv,
     m_send,
     m_recv,
 ):
@@ -90,6 +92,8 @@
     t_me = lax.axis_index("tensor")
     my_out = dp // inner
     my_in = dp % inner
+    me = my_in * outer + my_out
+    last = seqs - 1
     hid_pieces = pieces_of(hid_width)
     piece = hid_width // hid_pieces
     cut = 256 * ((piece // 256 + 1) // 2)
@@ -139,27 +143,40 @@
     def p_peer(k):
         return (my_out * inner + (my_in + k) % inner, t_me)
 
-    peers = [(t_peer, t_size), (z_peer, outer), (p_peer, inner)]
+    others = outer * inner - 1
+
+    def each_other(act):
+        def visit(n, carry):
+            act(((dp + 1 + (n + others // 2) % others) % (others + 1), t_me))
+            return carry
+
+        if others:
+            lax.fori_loop(0, others, visit, None)
+
     barrier = pltpu.get_barrier_semaphore()
-    for peer_of, count in peers:
-        for k in range(1, count):
-            pl.semaphore_signal(
-                barrier, inc=1, device_id=peer_of(k), device_id_type=pl.DeviceIdType.MESH
-            )
+
+    def greet(peer):
+        pl.semaphore_signal(
+            barrier, inc=1, device_id=peer, device_id_type=pl.DeviceIdType.MESH
+        )
+
+    for k in range(1, t_size):
+        greet(t_peer(k))
+    each_other(greet)
 
     for copy in small_copies:
         copy.wait()
     own_row = owner_row[...]
     lang_lane = lax.broadcasted_iota(jnp.int32, own_row.shape, 1)
-    sub = lax.broadcasted_iota(jnp.int32, places.shape[2:], 0)
-    place_block = jnp.full(places.shape[2:], -1, jnp.int32)
+    sub = lax.broadcasted_iota(jnp.int32, places.shape[1:], 0)
+    place_block = jnp.full(places.shape[1:], -1, jnp.int32)
     for s in range(seqs):
         lang = language[s]
         own = owner_list[lang]
         earlier = (own_row == own) & (lang_lane < lang)
         slot = jnp.sum(earlier.astype(jnp.int32), axis=1, keepdims=True)
         place_block = jnp.where(sub == s, own * slots + slot, place_block)
-    places[my_in, my_out] = place_block
+    places[me] = place_block
     sums[...] = jnp.zeros_like(sums)
     counts[...] = jnp.zeros_like(counts)
 
@@ -206,7 +223,15 @@
             0, hid_pieces, add_piece, jnp.zeros((tokens, rank), jnp.float32)
         )
         for k in range(1, t_size):
-            send(part.at[s], peer_part.at[s, k - 1], t_send.at[s], t_recv.at[s], t_peer(k))
+            for q in range(4):
+                some = pl.ds(q * (tokens // 4), tokens // 4)
+                send(
+                    part.at[s, some],
+                    peer_part.at[s, k - 1, some],
+                    t_send.at[s],
+                    t_recv.at[s],
+                    t_peer(k),
+                )
 
     first = t_me * half
     even = pl.ds(first, rows, stride=2)
@@ -241,41 +266,49 @@
             r_split[...],
             preferred_element_type=jnp.float32,
         )
-        gathered[s, my_in, my_out] = jnp.concatenate([pre[:rows], pre[rows:]], axis=1)
-        for k in range(1, outer):
-            block = gathered.at[s, my_in, my_out]
-            send(block, block, z_send.at[s], z_recv.at[s], z_peer(k))
+        gathered[s, me] = jnp.concatenate([pre[:rows], pre[rows:]], axis=1)
+        block = gathered.at[s, me]
+
+        @pl.when(s < last)
+        def _():
+            for k in range(1, outer):
+                send(block, block, z_send.at[s], z_recv.at[s], z_peer(k))
+
+        @pl.when(s == last)
+        def _():
+            each_other(lambda peer: send(block, block, d_send.at[0], d_recv.at[0], peer))
+
         out[slots + s] = jnp.concatenate([g_scr[even, :], g_scr[odd, :]], axis=1)
 
     def forward(s):
-        @pl.when(s == 0)
-        def _():
-            if outer > 1:
-                take(places.at[0, pl.ds(0, outer - 1)], m_recv.at[0])
-            for k in range(1, inner):
-                block = places.at[my_in]
-                send(block, block, m_send.at[1], m_recv.at[1], p_peer(k))
-
         if outer > 1:
-            take(gathered.at[s, 0, pl.ds(0, outer - 1)], z_recv.at[s])
+            take(gathered.at[s, pl.ds(0, outer - 1)], z_recv.at[s])
+        block = gathered.at[s, pl.ds(my_in * outer, outer)]
         for k in range(1, inner):
-            block = gathered.at[s, my_in]
             send(block, block, p_send.at[s], p_recv.at[s], p_peer(k))
 
     def accumulate(s):
-        if inner > 1:
+        if others:
 
             @pl.when(s == 0)
             def _():
-                take(places.at[pl.ds(0, inner - 1)], m_recv.at[1])
-
-            take(gathered.at[s, pl.ds(0, inner - 1)], p_recv.at[s])
+                take(places.at[pl.ds(0, others)], m_recv.at[0])
+
+            @pl.when(s == last)
+            def _():
+                take(gathered.at[last, pl.ds(0, others)], d_recv.at[0])
+
+        if inner > 1:
+
+            @pl.when(s < last)
+            def _():
+                take(gathered.at[s, pl.ds(0, (inner - 1) * outer)], p_recv.at[s])
 
         def add_block(i, held):
             total, seen = list(held[0]), list(held[1])
             for o in range(outer):
-                place = places[i, o, pl.ds(s, 1), :]
-                row = gathered[s, i, o]
+                place = places[i * outer + o, pl.ds(s, 1), :]
+                row = gathered[s, i * outer + o]
                 for j in range(slots):
                     hit = (place == dp * slots + j).astype(jnp.float32)
                     total[j] = total[j] + hit * row
@@ -297,10 +330,9 @@
 
     w_out_copy.wait()
     w_in_copy.wait()
-    pl.semaphore_wait(barrier, sum(count - 1 for _, count in peers))
-    for k in range(1, outer):
-        block = places.at[my_in, my_out]
-        send(block, block, m_send.at[0], m_recv.at[0], z_peer(k))
+    pl.semaphore_wait(barrier, t_size - 1 + others)
+    own_places = places.at[me]
+    each_other(lambda peer: send(own_places, own_places, m_send.at[0], m_recv.at[0], peer))
 
     left_rows = jnp.concatenate([left_inv[even, :], left_inv[odd, :]], axis=0)
     high, low = halves(left_rows)
@@ -317,7 +349,7 @@
         def _():
             reduce(i - 1)
 
-        @pl.when((i >= 2) & (i <= seqs + 1))
+        @pl.when((i >= 2) & (i <= seqs))
         def _():
             forward(i - 2)
 
@@ -334,14 +366,14 @@
     for s in range(seqs):
         if t_size > 1:
             take(peer_part.at[s], t_send.at[s])
+    for s in range(last):
         if outer > 1:
-            take(gathered.at[s, 0, pl.ds(0, outer - 1)], z_send.at[s])
+            take(gathered.at[s, pl.ds(0, outer - 1)], z_send.at[s])
         if inner > 1:
-            take(gathered.at[s, pl.ds(0, inner - 1)], p_send.at[s])
-    if outer > 1:
-        take(places.at[0, pl.ds(0, outer - 1)], m_send.at[0])
-    if inner > 1:
-        take(places.at[pl.ds(0, inner - 1)], m_send.at[1])
+            take(gathered.at[s, pl.ds(0, (inner - 1) * outer)], p_send.at[s])
+    if others:
+        take(gathered.at[last, pl.ds(0, others)], d_send.at[0])
+        take(places.at[pl.ds(0, others)], m_send.at[0])
 
 
 def per_device(hidden, out_grad, proj_in, proj_out, left_inv, right_inv, lengths, language, owner):
@@ -376,8 +408,8 @@
             pltpu.VMEM((rank, rank), jnp.float32),
             pltpu.VMEM((half, 3 * rank), jnp.bfloat16),
             pltpu.VMEM((3 * rank, rank), jnp.bfloat16),
-            pltpu.VMEM((seqs, inner, outer, rows, LANES), jnp.float32),
-            pltpu.VMEM((inner, outer, 8 * ((seqs + 7) // 8), LANES), jnp.int32),
+            pltpu.VMEM((seqs, dp_size, rows, LANES), jnp.float32),
+            pltpu.VMEM((dp_size, 8 * ((seqs + 7) // 8), LANES), jnp.int32),
             pltpu.VMEM((slots, rows, LANES), jnp.float32),
             pltpu.VMEM((8 * ((slots + 7) // 8), LANES), jnp.float32),
             pltpu.SMEM((seqs,), jnp.int32),
@@ -396,8 +428,10 @@
             dma((seqs,)),
             dma((seqs,)),
             dma((seqs,)),
-            dma((2,)),
-            dma((2,)),
+            dma((1,)),
+            dma((1,)),
+            dma((1,)),
+            dma((1,)),
         ],
         compiler_params=pltpu.CompilerParams(
             collective_id=0, has_side_effects=True, vmem_limit_bytes=64 * 1024 * 1024

time: 25.9 us -> 24.7 us (0.954)
  Pallas kernels: 25.1 us -> 23.9 us
    pallas_call x1, Pallas kernels: 23.6 us -> 22.4 us  [per_device(): pl.pallas_call(functools.partial(kernel, (t_size, outer, inner, slots)),...]
where the time goes in v5:
time: 24.7 us; the launch traced here: 24.6 us
  Pallas kernels  23.9 us (97%)
  between operations  0.64 us (3%)
    pallas_call x1, Pallas kernels, per_device(): pl.pallas_call(functools.partial(kernel, (t_size, outer, inner, slots)),...  22.4 us
    pallas_call x1, Pallas kernels, per_device(): pl.pallas_call(functools.partial(finish, slots), out_shape=(jax.ShapeDtyp...  1.56 us

profile of v5, /device:TPU:0, one launch (start us, length us, event | category | flops | bytes accessed | tf_op | source)
XLA Modules:
  0.0 24.6 jit_solution(1824657652049821770)
XLA Ops:
  0.6 22.4 %shard_map.104.rows_in = f32[10,16,128]{2,1,0:T(8,128)} custom-call(s32[3]{0:T(128)} %lengths_in.1, s32[3]{0:T(128)} %language_in.1, s32[100]{0:T(128)} %owner_in.1, s32[1,100]{1,0:T(1,128)} %bitcast.1, f32[64,64]{1,0:T(8,128)} %left_inv_in.1, f32[64,64]{1,0:T(8,128)} %right_inv_in.1, bf16[3,256,7168]{2,1,0:T(8,128)(2,1)} %hidden.1, ...), custom_call_target="tpu_custom_call" | custom-call | flops 905969664 | bytes 15335424 | tf_op jit(solution)/shard_map/pallas_call | solution.py:396
  23.0 1.6 %shard_map.105 = (f32[3,2048]{1,0:T(4,128)}, f32[7,2048]{1,0:T(8,128)}) custom-call(f32[10,16,128]{2,1,0:T(8,128)} %shard_map.104.rows_in), custom_call_target="tpu_custom_call" | custom-call | tf_op jit(solution)/shard_map/pallas_call | solution.py:456

commit v6 on v5

--- a/solution.py
+++ b/solution.py
@@ -201,8 +201,8 @@
         def _():
             og_copy(s + 1).start()
 
-        right = lax.dot_general(og[s], w_out[...], dims, preferred_element_type=jnp.float32)
-        part[s, :, rank:wide] = right
+        right = lax.dot_general(w_out[...], og[s], dims, preferred_element_type=jnp.float32)
+        part[s, rank:wide, :] = right
 
         def add_piece(c, left):
             hid_copy(s, c).wait()
@@ -215,16 +215,16 @@
             for begin, end in ((0, cut), (cut, piece)):
                 cols = pl.ds(base + begin, end - begin)
                 left += lax.dot_general(
-                    hid[s, :, cols], w_in[:, cols], dims, preferred_element_type=jnp.float32
+                    w_in[:, cols], hid[s, :, cols], dims, preferred_element_type=jnp.float32
                 )
             return left
 
-        part[s, :, 0:rank] = lax.fori_loop(
-            0, hid_pieces, add_piece, jnp.zeros((tokens, rank), jnp.float32)
+        part[s, 0:rank, :] = lax.fori_loop(
+            0, hid_pieces, add_piece, jnp.zeros((rank, tokens), jnp.float32)
         )
         for k in range(1, t_size):
             for q in range(4):
-                some = pl.ds(q * (tokens // 4), tokens // 4)
+                some = pl.ds(q * (wide // 4), wide // 4)
                 send(
                     part.at[s, some],
                     peer_part.at[s, k - 1, some],
@@ -243,12 +243,12 @@
         both = part[s]
         for k in range(1, t_size):
             both += peer_part[s, k - 1]
-        token = lax.broadcasted_iota(jnp.int32, both.shape, 0)
+        token = lax.broadcasted_iota(jnp.int32, both.shape, 1)
         both = jnp.where(token < lengths[s], both, 0.0)
         high, low = halves(both)
-        split = jnp.concatenate([high, low], axis=1)
+        split = jnp.concatenate([high, low], axis=0)
         full = lax.dot_general(
-            split, split, (((0,), (0,)), ((), ())), preferred_element_type=jnp.float32
+            split, split, (((1,), (1,)), ((), ())), preferred_element_type=jnp.float32
         )
         full = full[0:rank] + full[wide : wide + rank]
         full = full[:, 0:wide] + full[:, wide : 2 * wide]
@@ -403,8 +403,8 @@
             pltpu.VMEM((seqs, tokens, og_width), jnp.bfloat16),
             pltpu.VMEM((rank, hid_width), jnp.bfloat16),
             pltpu.VMEM((rank, og_width), jnp.bfloat16),
-            pltpu.VMEM((seqs, tokens, 2 * rank), jnp.float32),
-            pltpu.VMEM((seqs, max(t_size - 1, 1), tokens, 2 * rank), jnp.float32),
+            pltpu.VMEM((seqs, 2 * rank, tokens), jnp.float32),
+            pltpu.VMEM((seqs, max(t_size - 1, 1), 2 * rank, tokens), jnp.float32),
             pltpu.VMEM((rank, rank), jnp.float32),
             pltpu.VMEM((half, 3 * rank), jnp.bfloat16),
             pltpu.VMEM((3 * rank, rank), jnp.bfloat16),

time: 24.7 us -> 25 us (1.012)
  Pallas kernels: 23.9 us -> 24.2 us
    pallas_call x1, Pallas kernels: 22.4 us -> 22.6 us  [per_device(): pl.pallas_call(functools.partial(kernel, (t_size, outer, inner, slots)),...]
where the time goes in v6:
time: 25 us; the launch traced here: 24.8 us
  Pallas kernels  24.2 us (97%)
  between operations  0.64 us (3%)
    pallas_call x1, Pallas kernels, per_device(): pl.pallas_call(functools.partial(kernel, (t_size, outer, inner, slots)),...  22.6 us
    pallas_call x1, Pallas kernels, per_device(): pl.pallas_call(functools.partial(finish, slots), out_shape=(jax.ShapeDtyp...  1.56 us

profile of v6, /device:TPU:0, one launch (start us, length us, event | category | flops | bytes accessed | tf_op | source)
XLA Modules:
  0.0 24.8 jit_solution(12380741247731704307)
XLA Ops:
  0.6 22.6 %shard_map.104.rows_in = f32[10,16,128]{2,1,0:T(8,128)} custom-call(s32[3]{0:T(128)} %lengths_in.1, s32[3]{0:T(128)} %language_in.1, s32[100]{0:T(128)} %owner_in.1, s32[1,100]{1,0:T(1,128)} %bitcast.1, f32[64,64]{1,0:T(8,128)} %left_inv_in.1, f32[64,64]{1,0:T(8,128)} %right_inv_in.1, bf16[3,256,7168]{2,1,0:T(8,128)(2,1)} %hidden.1, ...), custom_call_target="tpu_custom_call" | custom-call | flops 905969664 | bytes 15335424 | tf_op jit(solution)/shard_map/pallas_call | solution.py:396
  23.3 1.6 %shard_map.105 = (f32[3,2048]{1,0:T(4,128)}, f32[7,2048]{1,0:T(8,128)}) custom-call(f32[10,16,128]{2,1,0:T(8,128)} %shard_map.104.rows_in), custom_call_target="tpu_custom_call" | custom-call | tf_op jit(solution)/shard_map/pallas_call | solution.py:456

commit v7 on v6

--- a/solution.py
+++ b/solution.py
@@ -205,6 +205,10 @@
         part[s, rank:wide, :] = right
 
         def add_piece(c, left):
+            @pl.when((c == hid_pieces // 2) & (s >= 2))
+            def _():
+                reduce(s - 2)
+
             hid_copy(s, c).wait()
 
             @pl.when(s + 1 < seqs)
@@ -340,26 +344,28 @@
     high, low = halves(right_inv[...])
     r_split[...] = jnp.concatenate([high, high, low], axis=0)
 
-    def step(i, carry):
-        @pl.when(i < seqs)
+    def project_step(s, carry):
+        project(s)
+        return carry
+
+    def reduce_step(s, carry):
+        reduce(s)
+
+        @pl.when(s >= 1)
         def _():
-            project(i)
-
-        @pl.when((i >= 1) & (i <= seqs))
-        def _():
-            reduce(i - 1)
-
-        @pl.when((i >= 2) & (i <= seqs))
-        def _():
-            forward(i - 2)
-
-        @pl.when(i >= 3)
-        def _():
-            accumulate(i - 3)
+            forward(s - 1)
 
         return carry
 
-    lax.fori_loop(0, seqs + 3, step, None)
+    def accumulate_step(s, carry):
+        accumulate(s)
+        return carry
+
+    lax.fori_loop(0, seqs, project_step, None)
+    for s in range(seqs - 3):
+        forward(s)
+    lax.fori_loop(max(seqs - 2, 0), seqs, reduce_step, None)
+    lax.fori_loop(0, seqs, accumulate_step, None)
     for j in range(slots):
         out[j] = sums[j] / jnp.maximum(counts[pl.ds(j, 1), :], 1.0)
 

time: 25 us -> 25.9 us (1.036)
  Pallas kernels: 24.2 us -> 25.1 us
    pallas_call x1, Pallas kernels: 22.6 us -> 23.5 us  [per_device(): pl.pallas_call(functools.partial(kernel, (t_size, outer, inner, slots)),...]
where the time goes in v7:
time: 25.9 us; the launch traced here: 25.7 us
  Pallas kernels  25.1 us (97%)
  between operations  0.64 us (2%)
    pallas_call x1, Pallas kernels, per_device(): pl.pallas_call(functools.partial(kernel, (t_size, outer, inner, slots)),...  23.5 us
    pallas_call x1, Pallas kernels, per_device(): pl.pallas_call(functools.partial(finish, slots), out_shape=(jax.ShapeDtyp...  1.56 us

profile of v7, /device:TPU:0, one launch (start us, length us, event | category | flops | bytes accessed | tf_op | source)
XLA Modules:
  0.0 25.7 jit_solution(9651664380218791085)
XLA Ops:
  0.6 23.5 %shard_map.104.rows_in = f32[10,16,128]{2,1,0:T(8,128)} custom-call(s32[3]{0:T(128)} %lengths_in.1, s32[3]{0:T(128)} %language_in.1, s32[100]{0:T(128)} %owner_in.1, s32[1,100]{1,0:T(1,128)} %bitcast.1, f32[64,64]{1,0:T(8,128)} %left_inv_in.1, f32[64,64]{1,0:T(8,128)} %right_inv_in.1, bf16[3,256,7168]{2,1,0:T(8,128)(2,1)} %hidden.1, ...), custom_call_target="tpu_custom_call" | custom-call | flops 905969664 | bytes 15335424 | tf_op jit(solution)/shard_map/pallas_call | solution.py:402
  24.2 1.6 %shard_map.105 = (f32[3,2048]{1,0:T(4,128)}, f32[7,2048]{1,0:T(8,128)}) custom-call(f32[10,16,128]{2,1,0:T(8,128)} %shard_map.104.rows_in), custom_call_target="tpu_custom_call" | custom-call | tf_op jit(solution)/shard_map/pallas_call | solution.py:462
